TPU v7x, 256 devices: a whole 4x4x8 slice. The times are simulated.
256 devices in a mesh: tm: 32 (over y_lo, z, core), blk: 8 (over x, y_hi).
Axes of the slice: x: 4, y: 4 (y_hi: 2, y_lo: 2; y = y_hi * 2 + y_lo), z: 8, core: 2. Of those that a mesh axis runs over, the one named last changes fastest.
Arguments:
- psi_start: float32 [32, 8, 6, 8192], P('tm', 'blk'), may hold values from -6 to 6
- objective: float32 [32, 8, 6, 8192], P('tm', 'blk'), may hold values from -6 to 6
- jacobian: bfloat16 [32, 8, 6, 6, 6, 8192], P('tm', 'blk'), may hold values from -1 to 1
- precond: bfloat16 [32, 8, 6, 6, 8192], P('tm', 'blk'), may hold values from -0.8984375 to 0.8984375
- volume: float32 [8, 8192], P('blk'), may hold values from 0.02 to 0.2
- counts: int32 [8], P('blk'), may hold values from 4096 to 8192, as said below
- neighbours: int32 [8, 6, 8192], P('blk'), may hold values from 0 to 255
- donor: int32 [8, 512], P('blk'), may hold values from 0 to 4095
- match_block: int32 [32, 8, 4], P('tm', 'blk'), may hold values from 0 to 31
- slide: int32 [32, 8, 4], P('tm', 'blk'), may hold values from 0 to 127
Outputs:
- psi: float32 [32, 8, 6, 8192], P('tm', 'blk')
Inputs may be any that keep to these rules, and one draw needn't show every extreme that they name: `counts`: every value lies in 4096 to 8192; some partition holds exactly 8192 live cells.
All inputs are finite; a program needn't handle non-finite values.
Results may differ from a plain program's by a relative error of at most 0.0004.
Values sent between devices are 32-bit elements; how exact they have to be, the bound alone decides.
No kernel may reach another device: no remote copies, remote signals or barrier semaphores. Data moves between devices by JAX's collectives and lax.ppermute only.
A program may use at most 64 MiB of HBM per device.

v0:
```python
import math

import jax
import jax.numpy as jnp
from jax import lax
from jax.sharding import PartitionSpec as P

SWEEPS = 2


def time_matrix(count):
    index = jnp.arange(count)
    offset = index[:, None] - index[None, :]
    angle = math.pi * offset.astype(jnp.float32) / count
    parity = jnp.where(offset % 2 == 0, 1.0, -1.0).astype(jnp.float32)
    safe_angle = jnp.where(offset == 0, 0.5 * math.pi, angle)
    sine = jnp.sin(safe_angle)
    value = 0.5 * parity * jnp.cos(safe_angle) / sine + 0.125 * parity / (sine * sine)
    diagonal_value = 0.25 * (count * count + 2) / 12.0
    return jnp.where(offset == 0, diagonal_value, value)


def face_source(match_block, slide):
    within = jnp.arange(128)
    full = match_block[..., None] * 128 + (within + slide[..., None]) % 128
    return full.reshape(-1)


def local(
    psi_start, objective, jacobian, precond, volume, counts, neighbours, donor, match_block, slide
):
    cells = psi_start.shape[3]
    fields = psi_start.shape[2]
    stencil_width = neighbours.shape[1]
    faces = donor.shape[1]
    face_blocks = faces // 128
    groups = cells // 128
    live = (jnp.arange(cells) < counts[0]).astype(jnp.float32)
    psi = psi_start[0, 0] * live[None, :]
    slices = lax.axis_size("tm")
    parts = lax.axis_size("blk")
    own_slice = lax.axis_index("tm")
    d = time_matrix(slices)
    column = lax.dynamic_index_in_dim(d, own_slice, 1, keepdims=False)
    source = face_source(match_block[0, 0], slide[0, 0])
    stencil = neighbours[0].reshape(stencil_width, groups, 128)
    half_cells = cells // 2
    donor_table = (jnp.arange(half_cells)[:, None] == donor[0][None, :]).astype(jnp.float32)
    ghost_table = (jnp.arange(parts * faces)[:, None] == source[None, :]).astype(jnp.float32)
    window_slot = jnp.arange(256)
    jac_local = jacobian[0, 0]
    pre_local = precond[0, 0]
    target = objective[0, 0]
    weights = volume[0]
    for sweep in range(SWEEPS):
        sent = jnp.dot(
            psi[:, :half_cells],
            donor_table,
            precision=lax.Precision.HIGHEST,
            preferred_element_type=jnp.float32,
        )
        pool = lax.all_gather(sent, "blk", axis=1, tiled=True)
        ghost = jnp.dot(
            pool, ghost_table, precision=lax.Precision.HIGHEST, preferred_element_type=jnp.float32
        )
        ghost_tiled = jnp.tile(
            ghost.reshape(fields, face_blocks, 128), (1, groups // face_blocks, 1)
        )
        window = jnp.concatenate([psi.reshape(fields, groups, 128), ghost_tiled], axis=2)
        gathered = []
        for slot in range(stencil_width):
            table = (window_slot[None, :, None] == stencil[slot][:, None, :]).astype(jnp.float32)
            picked = jnp.einsum("fgs,gsc->fgc", window, table, precision=lax.Precision.HIGHEST)
            gathered.append(picked.reshape(fields, cells))
        values = jnp.stack(gathered, axis=1)
        flux = jnp.sum(jac_local.astype(jnp.float32) * values[None], axis=(1, 2))
        coupling = jnp.einsum(
            "s,sfc->fc",
            column,
            lax.all_gather(psi[None], "tm", axis=0, tiled=True),
            precision=lax.Precision.HIGHEST,
        )
        residual = flux + weights[None, :] * coupling - target
        update = jnp.sum(pre_local.astype(jnp.float32) * residual[None], axis=1)
        psi = (psi - update) * live[None, :]
    return psi[None, None]


def solution(mesh):
    in_specs = (
        P("tm", "blk", None, None),
        P("tm", "blk", None, None),
        P("tm", "blk", None, None, None, None),
        P("tm", "blk", None, None, None),
        P("blk", None),
        P("blk"),
        P("blk", None, None),
        P("blk", None),
        P("tm", "blk", None),
        P("tm", "blk", None),
    )
    out_specs = P("tm", "blk", None, None)
    return jax.shard_map(local, mesh=mesh, in_specs=in_specs, out_specs=out_specs, check_vma=False)
```

profile of v0, /device:TPU:1, one launch (start us, length us, event | category | flops | bytes accessed | tf_op | source)
XLA Modules:
  0.0 188.9 jit_solution(16363947595417883786)
XLA Ops:
  6.5 0.0 copy-start.7
  6.5 0.0 copy-start.5
  6.5 0.0 all-gather.3.cloned.1.call-start
  7.2 1.1 bitcast_multiply_fusion.2
  8.3 0.8 copy.24
  9.2 0.0 all-gather.3.cloned.1.call-update
  9.2 0.0 all-gather.5.cloned.1.call-start
  9.2 1.1 fusion.46
  10.3 0.0 copy-start
  10.3 0.0 copy-start.3
  10.3 3.3 %fusion.17 = f32[6,512]{1,0:T(8,128)S(1)} fusion(s32[512]{0:T(512)} %bitcast.179, f32[6,8192]{1,0:T(8,128)S(1)} %fusion.46), kind=kOutput, calls=%fused_computation.38 | convolution fusion | flops 153092096 | bytes 145408 | tf_op jit(solution)/shard_map/dot_general | solution.py:56
  13.6 29.2 %all_gather.12 = f32[6,4096]{1,0:T(8,128)S(1)} all-gather(f32[6,512]{1,0:T(8,128)S(1)} %fusion.17), channel_id=1, replica_groups=mesh['tm'=32,'blk'=8] {'blk'}, dimensions={1}, use_global_device_ids=true | all-gather | bytes 110592 | tf_op jit(solution)/shard_map/all_gather | solution.py:62
  42.8 0.0 copy-done.7
  42.8 0.0 copy-done.5
  42.9 0.1 fusion.64
  42.9 2.5 %fusion.40 = f32[6,4,128]{2,0,1:T(8,128)S(1)} fusion(f32[6,4096]{1,0:T(8,128)S(1)} %all_gather.12, s32[512]{0:T(512)S(1)} %fusion.64), kind=kOutput, calls=%fused_computation.64 | convolution fusion | flops 153092096 | bytes 112640 | tf_op jit(solution)/shard_map/dot_general | solution.py:63
  45.5 0.0 copy-done
  45.5 0.1 copy_multiply_fusion.1
  45.6 0.0 copy-done.3
  45.7 2.8 %fusion.13 = f32[6,6,8192]{2,0,1:T(8,128)S(1)} fusion(s32[64,128]{1,0:T(8,128)S(1)} %bitcast.176, f32[6,64,128]{2,0,1:T(8,128)S(1)} %bitcast.158, f32[6,64,128]{2,0,1:T(8,128)S(1)} %copy_multiply_fusion.1), kind=kOutput, calls=%fused_computation.27 | convolution fusion | flops 153190400 | bytes 688128 | tf_op jit(solution)/shard_map/fgs,gsc->fgc/dot_general | solution.py:73
  48.5 2.8 %fusion.12 = f32[6,6,8192]{2,0,1:T(8,128)S(1)} fusion(f32[6,6,8192]{2,0,1:T(8,128)S(1)} %fusion.13, s32[64,128]{1,0:T(8,128)S(1)} %bitcast.174, f32[6,64,128]{2,0,1:T(8,128)S(1)} %bitcast.159, f32[6,64,128]{2,0,1:T(8,128)S(1)} %copy_multiply_fusion.1), kind=kOutput, calls=%fused_computation.25 | convolution fusion | flops 153190400 | bytes 819200 | tf_op jit(solution)/shard_map/fgs,gsc->fgc/dot_general | solution.py:73
  51.3 2.8 %fusion.11 = f32[6,6,8192]{2,0,1:T(8,128)S(1)} fusion(f32[6,6,8192]{2,0,1:T(8,128)S(1)} %fusion.12, s32[64,128]{1,0:T(8,128)S(1)} %bitcast.172, f32[6,64,128]{2,0,1:T(8,128)S(1)} %bitcast.160, f32[6,64,128]{2,0,1:T(8,128)S(1)} %copy_multiply_fusion.1), kind=kOutput, calls=%fused_computation.23 | convolution fusion | flops 153190400 | bytes 819200 | tf_op jit(solution)/shard_map/fgs,gsc->fgc/dot_general | solution.py:73
  54.1 3.2 %fusion.10 = f32[6,6,8192]{2,0,1:T(8,128)S(1)} fusion(f32[6,6,8192]{2,0,1:T(8,128)S(1)} %fusion.11, s32[64,128]{1,0:T(8,128)S(1)} %bitcast.170, f32[6,64,128]{2,0,1:T(8,128)S(1)} %bitcast.161, f32[6,64,128]{2,0,1:T(8,128)S(1)} %copy_multiply_fusion.1), kind=kOutput, calls=%fused_computation.21 | convolution fusion | flops 153190400 | bytes 819200 | tf_op jit(solution)/shard_map/fgs,gsc->fgc/dot_general | solution.py:73
  57.3 2.8 %fusion.9 = f32[6,6,8192]{2,0,1:T(8,128)S(1)} fusion(f32[6,6,8192]{2,0,1:T(8,128)S(1)} %fusion.10, s32[64,128]{1,0:T(8,128)S(1)} %bitcast.168, f32[6,64,128]{2,0,1:T(8,128)S(1)} %bitcast.162, f32[6,64,128]{2,0,1:T(8,128)S(1)} %copy_multiply_fusion.1), kind=kOutput, calls=%fused_computation.19 | convolution fusion | flops 153190400 | bytes 819200 | tf_op jit(solution)/shard_map/fgs,gsc->fgc/dot_general | solution.py:73
  60.1 2.8 %fusion.8 = f32[6,6,8192]{2,0,1:T(8,128)S(1)} fusion(f32[6,6,8192]{2,0,1:T(8,128)S(1)} %fusion.9, s32[64,128]{1,0:T(8,128)S(1)} %bitcast.166, f32[6,64,128]{2,0,1:T(8,128)S(1)} %bitcast.163, f32[6,64,128]{2,0,1:T(8,128)S(1)} %copy_multiply_fusion.1), kind=kOutput, calls=%fused_computation.17 | convolution fusion | flops 153190400 | bytes 819200 | tf_op jit(solution)/shard_map/fgs,gsc->fgc/dot_general | solution.py:73
  63.0 0.7 copy.23
  63.7 4.0 %fusion = f32[6,8192]{1,0:T(8,128)S(1)} fusion(bf16[1,1,6,6,6,8192]{5,4,3,2,1,0:T(8,128)(2,1)} %param.12, f32[6,6,8192]{2,1,0:T(8,128)S(1)} %copy.23), kind=kLoop, calls=%fused_computation.2 | loop fusion | flops 5259264 | bytes 4915200 | tf_op jit(solution)/shard_map/reduce_sum | solution.py:76
  67.7 18.0 %all-gather.3.cloned.1.call-done = f32[32,6,8192]{2,1,0:T(8,128)} async-done(((f32[1,6,8192]{2,1,0:T(8,128)}), f32[32,6,8192]{2,1,0:T(8,128)}) %all-gather.3.cloned.1.call-update) | async-done | bytes 6291472 | tf_op jit(solution)/shard_map/all_gather | solution.py:80
  85.7 0.0 copy-start.2
  85.7 0.0 copy-start.4
  85.7 0.0 copy-start.1
  85.7 9.9 %fusion.20 = f32[1,6,8192]{2,0,1:T(1,128)S(1)} fusion(f32[32,6,8192]{2,1,0:T(8,128)} %all-gather.3.cloned.1.call-done, f32[32,32]{0,1:T(8,128)S(1)} %convert_multiply_fusion.4, s32[]{:T(128)S(6)} %select_n.37, pred[32,32]{0,1:T(8,128)(4,1)S(1)} %get-tuple-element.12, pred[32,32]{0,1:T(8,128)(4,1)S(1)} %get-tuple-element.11), kind=kOutput, calls=%fused_computation.42 | convolution fusion | flops 18874688 | bytes 6489604 | tf_op jit(solution)/shard_map/s,sfc->fc/dot_general | solution.py:77
  95.7 0.0 copy-start.6
  95.7 0.0 copy-done.2
  95.7 0.0 copy-done.4
  95.7 0.2 bitcast_subtract_fusion.1
  96.0 0.0 copy-done.1
  96.0 0.5 fusion.38
  96.5 0.2 subtract_multiply_fusion
  96.7 0.8 copy.27
  97.6 0.0 all-gather.5.cloned.1.call-update
  97.6 0.0 copy-done.6
  97.6 2.6 %fusion.16 = f32[6,512]{1,0:T(8,128)S(1)} fusion(s32[512]{0:T(512)S(1)} %bitcast.180, f32[6,8192]{1,0:T(8,128)S(1)} %fusion.38, f32[6,8192]{1,0:T(8,128)S(1)} %fusion.46, f32[4096]{0:T(1024)S(1)} %slice.47), kind=kOutput, calls=%fused_computation.37 | convolution fusion | flops 153141248 | bytes 292864 | tf_op jit(solution)/shard_map/dot_general | solution.py:56
  100.2 28.4 %all_gather.14 = f32[6,4096]{1,0:T(8,128)S(1)} all-gather(f32[6,512]{1,0:T(8,128)S(1)} %fusion.16), channel_id=1, replica_groups=mesh['tm'=32,'blk'=8] {'blk'}, dimensions={1}, use_global_device_ids=true | all-gather | bytes 110592 | tf_op jit(solution)/shard_map/all_gather | solution.py:62
  128.6 2.5 %fusion.41 = f32[6,4,128]{2,0,1:T(8,128)S(1)} fusion(f32[6,4096]{1,0:T(8,128)S(1)} %all_gather.14, s32[512]{0:T(512)S(1)} %fusion.64), kind=kOutput, calls=%fused_computation.65 | convolution fusion | flops 153092096 | bytes 112640 | tf_op jit(solution)/shard_map/dot_general | solution.py:63
  131.1 0.2 fusion.48
  131.3 2.8 %fusion.7 = f32[6,6,8192]{2,0,1:T(8,128)S(1)} fusion(s32[64,128]{1,0:T(8,128)S(1)} %bitcast.177, f32[6,64,128]{2,0,1:T(8,128)S(1)} %bitcast.152, f32[6,64,128]{2,0,1:T(8,128)S(1)} %fusion.48), kind=kOutput, calls=%fused_computation.15 | convolution fusion | flops 153190400 | bytes 688128 | tf_op jit(solution)/shard_map/fgs,gsc->fgc/dot_general | solution.py:73
  134.1 2.8 %fusion.6 = f32[6,6,8192]{2,0,1:T(8,128)S(1)} fusion(f32[6,6,8192]{2,0,1:T(8,128)S(1)} %fusion.7, s32[64,128]{1,0:T(8,128)S(1)} %bitcast.175, f32[6,64,128]{2,0,1:T(8,128)S(1)} %bitcast.153, f32[6,64,128]{2,0,1:T(8,128)S(1)} %fusion.48), kind=kOutput, calls=%fused_computation.13 | convolution fusion | flops 153190400 | bytes 819200 | tf_op jit(solution)/shard_map/fgs,gsc->fgc/dot_general | solution.py:73
  136.9 2.8 %fusion.5 = f32[6,6,8192]{2,0,1:T(8,128)S(1)} fusion(f32[6,6,8192]{2,0,1:T(8,128)S(1)} %fusion.6, s32[64,128]{1,0:T(8,128)S(1)} %bitcast.173, f32[6,64,128]{2,0,1:T(8,128)S(1)} %bitcast.154, f32[6,64,128]{2,0,1:T(8,128)S(1)} %fusion.48), kind=kOutput, calls=%fused_computation.11 | convolution fusion | flops 153190400 | bytes 819200 | tf_op jit(solution)/shard_map/fgs,gsc->fgc/dot_general | solution.py:73
  139.8 3.0 %fusion.4 = f32[6,6,8192]{2,0,1:T(8,128)S(1)} fusion(f32[6,6,8192]{2,0,1:T(8,128)S(1)} %fusion.5, s32[64,128]{1,0:T(8,128)S(1)} %bitcast.171, f32[6,64,128]{2,0,1:T(8,128)S(1)} %bitcast.155, f32[6,64,128]{2,0,1:T(8,128)S(1)} %fusion.48), kind=kOutput, calls=%fused_computation.9 | convolution fusion | flops 153190400 | bytes 819200 | tf_op jit(solution)/shard_map/fgs,gsc->fgc/dot_general | solution.py:73
  142.8 0.0 slice-start
  142.8 2.8 %fusion.3 = f32[6,6,8192]{2,0,1:T(8,128)S(1)} fusion(f32[6,6,8192]{2,0,1:T(8,128)S(1)} %fusion.4, s32[64,128]{1,0:T(8,128)S(1)} %bitcast.169, f32[6,64,128]{2,0,1:T(8,128)S(1)} %bitcast.156, f32[6,64,128]{2,0,1:T(8,128)S(1)} %fusion.48), kind=kOutput, calls=%fused_computation.7 | convolution fusion | flops 153190400 | bytes 819200 | tf_op jit(solution)/shard_map/fgs,gsc->fgc/dot_general | solution.py:73
  145.6 0.0 slice-start.1
  145.6 2.8 %fusion.2 = f32[6,6,8192]{2,0,1:T(8,128)S(1)} fusion(f32[6,6,8192]{2,0,1:T(8,128)S(1)} %fusion.3, s32[64,128]{1,0:T(8,128)S(1)} %bitcast.167, f32[6,64,128]{2,0,1:T(8,128)S(1)} %bitcast.157, f32[6,64,128]{2,0,1:T(8,128)S(1)} %fusion.48), kind=kOutput, calls=%fused_computation.5 | convolution fusion | flops 153190400 | bytes 819200 | tf_op jit(solution)/shard_map/fgs,gsc->fgc/dot_general | solution.py:73
  148.4 0.7 copy.26
  149.1 0.0 slice-done
  149.2 0.0 slice-done.1
  149.2 1.5 fusion.1
  150.7 19.2 %all-gather.5.cloned.1.call-done = f32[32,6,8192]{2,1,0:T(8,128)} async-done(((f32[1,6,8192]{2,1,0:T(8,128)}), f32[32,6,8192]{2,1,0:T(8,128)}) %all-gather.5.cloned.1.call-update) | async-done | bytes 6291472 | tf_op jit(solution)/shard_map/all_gather | solution.py:80
  169.9 10.1 %fusion.18 = f32[1,6,8192]{2,0,1:T(1,128)S(1)} fusion(f32[32,6,8192]{2,1,0:T(8,128)} %all-gather.5.cloned.1.call-done, f32[32,32]{0,1:T(8,128)S(1)} %convert_multiply_fusion.4, s32[]{:T(128)S(6)} %select_n.37, pred[32,32]{0,1:T(8,128)(4,1)S(1)} %get-tuple-element.12, pred[32,32]{0,1:T(8,128)(4,1)S(1)} %get-tuple-element.11), kind=kOutput, calls=%fused_computation.40 | convolution fusion | flops 18874688 | bytes 6489604 | tf_op jit(solution)/shard_map/s,sfc->fc/dot_general | solution.py:77
  180.0 0.2 bitcast_subtract_fusion
  180.2 0.5 fusion.39
  180.8 0.2 fusion.45
  180.9 0.9 copy.28
  (10 shorter events, 0.1 us)
Async XLA Ops:
  6.5 36.3 %copy-start.7 = (s32[1,1,4]{2,1,0:T(1,128)S(1)}, s32[1,1,4]{2,1,0:T(1,128)}, u32[]{:S(2)}) copy-start(s32[1,1,4]{2,1,0:T(1,128)} %param.18) | copy-start | bytes 52
  6.5 36.3 %copy-start.5 = (s32[1,1,4]{2,1,0:T(1,128)S(1)}, s32[1,1,4]{2,1,0:T(1,128)}, u32[]{:S(2)}) copy-start(s32[1,1,4]{2,1,0:T(1,128)} %param.19) | copy-start | bytes 52
  6.5 79.2 %all-gather.3.cloned.1.call-start = ((), (), s32[]{:S(2)}) async-start(), calls=%async_computation | async-start | bytes 8650752 | tf_op jit(solution)/shard_map/all_gather | solution.py:80
  9.2 160.7 %all-gather.5.cloned.1.call-start = ((), (), s32[]{:S(2)}) async-start(), calls=%async_computation.1 | async-start | bytes 8650752 | tf_op jit(solution)/shard_map/all_gather | solution.py:80
  10.3 35.2 %copy-start = (f32[1,1,6,8192]{3,1,2,0:T(1,128)S(1)}, f32[1,1,6,8192]{3,1,2,0:T(1,128)}, u32[]{:S(2)}) copy-start(f32[1,1,6,8192]{3,1,2,0:T(1,128)} %param.10) | copy-start | bytes 589828
  10.3 35.3 %copy-start.3 = (s32[1,6,8192]{2,0,1:T(1,128)S(1)}, s32[1,6,8192]{2,0,1:T(1,128)}, u32[]{:S(2)}) copy-start(s32[1,6,8192]{2,0,1:T(1,128)} %param.16) | copy-start | bytes 589828
  85.7 9.9 %copy-start.2 = (f32[1,1,6,8192]{3,1,2,0:T(1,128)S(1)}, f32[1,1,6,8192]{3,1,2,0:T(1,128)}, u32[]{:S(2)}) copy-start(f32[1,1,6,8192]{3,1,2,0:T(1,128)} %param.11) | copy-start | bytes 589828
  85.7 9.9 %copy-start.4 = (f32[1,8192]{1,0:T(1,128)S(1)}, f32[1,8192]{1,0:T(1,128)}, u32[]{:S(2)}) copy-start(f32[1,8192]{1,0:T(1,128)} %param.14) | copy-start | bytes 98308
  85.7 10.2 %copy-start.1 = (bf16[1,1,6,6,8192]{4,3,2,1,0:T(8,128)(2,1)S(1)}, bf16[1,1,6,6,8192]{4,3,2,1,0:T(8,128)(2,1)}, u32[]{:S(2)}) copy-start(bf16[1,1,6,6,8192]{4,3,2,1,0:T(8,128)(2,1)} %param.13) | copy-start | bytes 1769476
  95.7 1.9 %copy-start.6 = (s32[1,512]{1,0:T(1,128)S(1)}, s32[1,512]{1,0:T(1,128)}, u32[]{:S(2)}) copy-start(s32[1,512]{1,0:T(1,128)} %param.17) | copy-start | bytes 6148
  142.8 6.4 %slice-start = ((s8[4718592]{0:T(1024)(128)(4,1)}), s8[4194304]{0:T(1024)(128)(4,1)S(1)}, s32[]{:S(2)}) async-start(s8[4718592]{0:T(1024)(128)(4,1)} %bitcast.148), calls=%async_computation.2 | async-start | bytes 8388608
  145.6 3.6 %slice-start.1 = ((s8[4718592]{0:T(1024)(128)(4,1)}), s8[524288]{0:T(1024)(128)(4,1)S(1)}, s32[]{:S(2)}) async-start(s8[4718592]{0:T(1024)(128)(4,1)} %bitcast.148), calls=%async_computation.3 | async-start | bytes 1048576
Sparse Core Ops, SparseCore 0:
  9.3 76.3 all-gather.2
  97.7 72.1 all-gather.4
where the time goes:
time: 192 us; the launch traced here: 189 us
  matrix products  65.2 us (34%)
  blocking collectives  57.7 us (30%)
  waiting for transfers between devices  37.3 us (19%)
  between operations  14.6 us (8%)
  other arithmetic  9.97 us (5%)
  local copies, waits for them, and re-layouts  4.11 us (2%)
    all_gather x2, blocking collectives, local(): pool = lax.all_gather(sent, 'blk', axis=1, tiled=True)  57.7 us
    all_gather x2, waiting for transfers between devices, local(): lax.all_gather(psi[None], 'tm', axis=0, tiled=True)  37.2 us
    dot_general x12, matrix products, local(): jnp.einsum('fgs,gsc->fgc', window, table, precision=lax.Precision.HIGHEST)  34.4 us
    dot_general x2, matrix products, local(): jnp.einsum('s,sfc->fc', column, lax.all_gather(psi[None], 'tm', axis=0, t...  20 us
    dot_general x2, matrix products, local(): jnp.dot(psi[:, :half_cells], donor_table, precision=lax.Precision.HIGHEST...  5.84 us
    reduce_sum x2, other arithmetic, local(): flux = jnp.sum(jac_local.astype(jnp.float32) * values[None], axis=(1, 2))  5.53 us
    dot_general x2, matrix products, local(): jnp.dot(pool, ghost_table, precision=lax.Precision.HIGHEST, preferred_ele...  5.07 us
  transfers between devices with their start and end apart: 2, of which 2 were waited for; matrix products, arithmetic and copies ran while one was open for 28% of the time, Pallas kernels for 0%

commit v1 on v0

v1 whole, which is shorter than its diff:
```python
import math

import numpy as np
import jax
import jax.numpy as jnp
from jax import lax
from jax.experimental import pallas as pl
from jax.experimental.pallas import tpu as pltpu
from jax.sharding import PartitionSpec as P

SWEEPS = 2
F = 6
K = 6
CELLS = 8192
GROUPS = 64
ROWS = F * GROUPS
NT = 32
CHIPS = 16
CHUNK = ROWS // CHIPS
VMEM = pl.BlockSpec(memory_space=pltpu.VMEM)
SMEM = pl.BlockSpec(memory_space=pltpu.SMEM)
ANY = pl.BlockSpec(memory_space=pl.ANY)


def time_kernel():
    n = np.arange(NT)
    parity = np.where(n % 2 == 0, 1.0, -1.0)
    angle = np.where(n == 0, 0.5 * math.pi, math.pi * n / NT)
    sine = np.sin(angle)
    value = 0.5 * parity * np.cos(angle) / sine + 0.125 * parity / (sine * sine)
    return np.where(n == 0, 0.25 * (NT * NT + 2) / 12.0, value).astype(np.float32)


def params(mib=12):
    return pltpu.CompilerParams(vmem_limit_bytes=mib * 1024 * 1024)


def cost(flops, nbytes):
    return pl.CostEstimate(flops=flops, bytes_accessed=nbytes, transcendentals=0)


def f32_rows(n):
    return jax.ShapeDtypeStruct((n, 128), jnp.float32)


def i32_rows(n):
    return jax.ShapeDtypeStruct((n, 128), jnp.int32)


def lane_gather(data, index):
    return jnp.take_along_axis(data, index, axis=1, mode="promise_in_bounds")


def tile(start):
    return pl.ds(pl.multiple_of(start, 8), 8)


def fetch_donor_kernel(psi_hbm, donor_hbm, sent_ref, psi_ref, donor_ref, sems):
    copies = [pltpu.make_async_copy(donor_hbm, donor_ref, sems.at[0]), pltpu.make_async_copy(psi_hbm, psi_ref, sems.at[1])]
    for copy in copies:
        copy.start()
    for copy in copies:
        copy.wait()
    donor_kernel(psi_ref, donor_ref, sent_ref)


def donor_kernel(psi_ref, donor_ref, sent_ref):
    sublane = lax.broadcasted_iota(jnp.int32, (8, 128), 0)

    def block(q, carry):
        donor = jnp.broadcast_to(donor_ref[pl.ds(q, 1), :], (8, 128))
        lane = donor & 127
        home = (donor >> 7) - sublane
        rows = []
        for f in range(F):
            total = jnp.zeros((8, 128), jnp.float32)
            for b in range(4):
                picked = lane_gather(psi_ref[pl.ds(f * GROUPS + b * 8, 8), :], lane)
                total = total + jnp.where(home == b * 8, picked, 0.0)
            rows.append(jnp.sum(total, axis=0, keepdims=True))
        rows.append(jnp.zeros((2, 128), jnp.float32))
        sent_ref[tile(q * 8), :] = jnp.concatenate(rows, axis=0)
        return carry

    lax.fori_loop(0, 4, block, 0, unroll=2)


def pack_donors(fetch, psi, donor):
    scratch = [pltpu.VMEM((ROWS, 128), jnp.float32), pltpu.VMEM((4, 128), jnp.int32), pltpu.SemaphoreType.DMA((2,))]
    return pl.pallas_call(
        fetch_donor_kernel if fetch else donor_kernel,
        out_shape=f32_rows(32),
        in_specs=[ANY, ANY] if fetch else [VMEM, VMEM],
        out_specs=VMEM,
        scratch_shapes=scratch if fetch else [],
        compiler_params=params(58 if fetch else 12),
        cost_estimate=cost(400000, 220000),
        name="pack_donors",
    )(psi, donor)


def merge_kernel(*refs):
    for n in range(4):
        refs[4][pl.ds(n * 32, 32), :] = refs[n][...]


def merge(*pieces):
    return pl.pallas_call(
        merge_kernel,
        out_shape=f32_rows(128),
        in_specs=[VMEM] * 4,
        out_specs=VMEM,
        compiler_params=params(),
        cost_estimate=cost(30000000000, 130000),
        name="merge",
    )(*pieces)


def prepare_kernel(
    counts_hbm, match_hbm, slide_hbm, pre_hbm, nbr_hbm, volume_hbm,
    dense_ref, stencil_ref, live_ref, scale_ref, route_ref,
    pre_ref, nbr_ref, volume_ref, counts_ref, match_ref, slide_ref, sems
):
    scalars = [
        pltpu.make_async_copy(counts_hbm, counts_ref, sems.at[3]),
        pltpu.make_async_copy(match_hbm, match_ref, sems.at[4]),
        pltpu.make_async_copy(slide_hbm, slide_ref, sems.at[5]),
    ]
    copies = [
        pltpu.make_async_copy(nbr_hbm, nbr_ref, sems.at[0]),
        pltpu.make_async_copy(volume_hbm, volume_ref, sems.at[1]),
        pltpu.make_async_copy(pre_hbm, pre_ref, sems.at[2]),
    ]
    for copy in scalars + copies:
        copy.start()
    for copy in scalars:
        copy.wait()
    own = lax.axis_index("blk")
    sublane = lax.broadcasted_iota(jnp.int32, (8, 128), 0)
    lane = lax.broadcasted_iota(jnp.int32, (8, 128), 1)
    place = jnp.zeros((8, 128), jnp.int32)
    turn = jnp.zeros((8, 128), jnp.int32)
    for q in range(4):
        block = match_ref[q]
        part = block // 4
        hop = (part // 2) ^ (own // 2)
        side = lax.rem(part, 2) ^ lax.rem(own, 2)
        place = jnp.where(sublane == q, side * 16 + hop * 4 + lax.rem(block, 4), place)
        turn = jnp.where(sublane == q, slide_ref[q], turn)
    route_ref[pl.ds(0, 8), :] = place
    route_ref[pl.ds(8, 8), :] = (lane + turn) & 127
    stencil_ref[...] = jnp.zeros_like(stencil_ref)
    copies[0].wait()
    for k in range(K):
        for b in range(8):
            stencil_ref[pl.ds(b * 64 + k, 8, stride=8), :] = nbr_ref[pl.ds(k * GROUPS + b * 8, 8), :]
    copies[1].wait()
    for b in range(8):
        live = jnp.where(sublane * 128 + lane + b * 1024 < counts_ref[0], 1.0, 0.0)
        live_ref[pl.ds(b * 8, 8), :] = live
        scale_ref[pl.ds(b * 8, 8), :] = live * volume_ref[pl.ds(b * 8, 8), :]
    copies[2].wait()

    def step(g, carry):
        at = pl.multiple_of(g * 128, 128)
        for i in range(F):
            dense_ref[pl.ds(i * F * GROUPS + g, F, stride=GROUPS), :] = pre_ref[i, :, pl.ds(at, 128)].astype(jnp.float32)
        return carry

    lax.fori_loop(0, GROUPS, step, 0, unroll=4)


def prepare(counts, match, slide, precond, neighbours, volume):
    return pl.pallas_call(
        prepare_kernel,
        out_shape=(f32_rows(F * F * GROUPS), i32_rows(GROUPS * 8), f32_rows(GROUPS), f32_rows(GROUPS), i32_rows(16)),
        in_specs=[ANY] * 6,
        out_specs=(VMEM,) * 5,
        scratch_shapes=[
            pltpu.VMEM((F, F, CELLS), jnp.bfloat16),
            pltpu.VMEM((ROWS, 128), jnp.int32),
            pltpu.VMEM((GROUPS, 128), jnp.float32),
            pltpu.SMEM((1,), jnp.int32),
            pltpu.SMEM((4,), jnp.int32),
            pltpu.SMEM((4,), jnp.int32),
            pltpu.SemaphoreType.DMA((6,)),
        ],
        compiler_params=params(58),
        cost_estimate=cost(1000000, 2500000),
        name="prepare",
    )(counts, match, slide, precond, neighbours, volume)


def flux_kernel(
    psi_hbm, target_hbm, jac_hbm, near_ref, far_ref, route_ref, live_ref, stencil_ref, dense_ref,
    out_ref, psi_s, target_s, jac_s, ghost_s, part_s, sems
):
    first = pltpu.make_async_copy(psi_hbm, psi_s, sems.at[8])
    first.start()

    def jac_copy(b):
        cells = pl.ds(pl.multiple_of(b * 1024, 1024), 1024)
        return pltpu.make_async_copy(jac_hbm.at[:, :, :, cells], jac_s.at[:, :, :, cells], sems.at[b])

    for b in range(8):
        jac_copy(b).start()
    last = pltpu.make_async_copy(target_hbm, target_s, sems.at[9])
    last.start()
    for q in range(4):
        place = jnp.broadcast_to(route_ref[pl.ds(q, 1), :], (8, 128))
        source = jnp.zeros((8, 128), jnp.float32)
        for n in range(16):
            source = jnp.where(place == n, near_ref[pl.ds(n * 8, 8), :], source)
            source = jnp.where(place == 16 + n, far_ref[pl.ds(n * 8, 8), :], source)
        turn = jnp.broadcast_to(route_ref[pl.ds(8 + q, 1), :], (8, 128))
        ghost_s[pl.ds(q * 8, 8), :] = lane_gather(source, turn)
    first.wait()
    for b in range(8):
        live = live_ref[pl.ds(b * 8, 8), :]
        for f in range(F):
            rows = pl.ds(f * GROUPS + b * 8, 8)
            psi_s[rows, :] = psi_s[rows, :] * live

    def step(b, carry):
        jac_copy(b).wait()
        for s in range(8):
            g = b * 8 + s
            at = pl.multiple_of(g * 128, 128)
            index = stencil_ref[tile(g * 8), :]
            outside = index >= 128
            pick = index & 127
            total = [None] * F
            for j in range(F):
                inner = jnp.broadcast_to(psi_s[pl.ds(j * GROUPS + g, 1), :], (8, 128))
                outer = jnp.broadcast_to(ghost_s[pl.ds((s % 4) * 8 + j, 1), :], (8, 128))
                value = jnp.where(outside, lane_gather(outer, pick), lane_gather(inner, pick))[:K]
                for i in range(F):
                    term = jac_s[i, j, :, pl.ds(at, 128)].astype(jnp.float32) * value
                    total[i] = term if j == 0 else total[i] + term
            for i in range(F):
                part_s[pl.ds(pl.multiple_of(g * 48 + i * 8, 8), K), :] = total[i]
        return carry

    lax.fori_loop(0, 8, step, 0)
    last.wait()

    def finish(b, carry):
        live = live_ref[tile(b * 8), :]
        residual = []
        for j in range(F):
            flux = part_s[pl.ds(b * 384 + j * 8, 8, stride=48), :]
            for k in range(1, K):
                flux = flux + part_s[pl.ds(b * 384 + j * 8 + k, 8, stride=48), :]
            residual.append(flux - target_s[tile(j * GROUPS + b * 8), :])
        for i in range(F):
            rows = tile(i * GROUPS + b * 8)
            value = psi_s[rows, :]
            for j in range(F):
                value = value - dense_ref[tile((i * F + j) * GROUPS + b * 8), :] * residual[j]
            out_ref[rows, :] = live * value
        return carry

    lax.fori_loop(0, 8, finish, 0)


def flux_part(psi, target, jac, near, far, route, live, stencil, dense):
    return pl.pallas_call(
        flux_kernel,
        out_shape=f32_rows(ROWS),
        in_specs=[ANY] * 3 + [VMEM] * 6,
        out_specs=VMEM,
        scratch_shapes=[
            pltpu.VMEM((ROWS, 128), jnp.float32),
            pltpu.VMEM((ROWS, 128), jnp.float32),
            pltpu.VMEM((F, F, K, CELLS), jnp.bfloat16),
            pltpu.VMEM((32, 128), jnp.float32),
            pltpu.VMEM((GROUPS * 48, 128), jnp.float32),
            pltpu.SemaphoreType.DMA((10,)),
        ],
        compiler_params=params(50),
        cost_estimate=cost(30000000000, 7000000),
        name="flux_part",
    )(psi, target, jac, near, far, route, live, stencil, dense)


def couple_kernel(own_ref, other_ref, out_ref):
    f = [float(v) for v in time_kernel()]
    first = lax.rem(lax.axis_index("tm"), 2) == 0
    even = f[0::2]
    odd = [jnp.where(first, f[2 * n + 1], f[2 * n - 1]) for n in range(CHIPS)]
    for t0 in range(0, CHIPS, 8):
        for r in range(CHUNK // 8):
            total = [None] * 8
            for s in range(CHIPS):
                own = own_ref[pl.ds(s * CHUNK + r * 8, 8), :]
                other = other_ref[pl.ds(s * CHUNK + r * 8, 8), :]
                for t in range(8):
                    n = (s - t0 - t) % CHIPS
                    term = even[n] * own + odd[n] * other
                    total[t] = term if s == 0 else total[t] + term
            for t in range(8):
                out_ref[pl.ds((t0 + t) * CHUNK + r * 8, 8), :] = total[t]


def couple(own, other):
    return pl.pallas_call(
        couple_kernel,
        out_shape=f32_rows(ROWS),
        in_specs=[VMEM, VMEM],
        out_specs=VMEM,
        compiler_params=params(),
        cost_estimate=cost(3200000, 600000),
        name="couple",
    )(own, other)


def finish_kernel(base_ref, coupling_ref, scale_ref, dense_ref, out_ref):
    def step(b, carry):
        scale = scale_ref[tile(b * 8), :]
        term = [scale * coupling_ref[tile(j * GROUPS + b * 8), :] for j in range(F)]
        for i in range(F):
            rows = tile(i * GROUPS + b * 8)
            value = base_ref[rows, :]
            for j in range(F):
                value = value - dense_ref[tile((i * F + j) * GROUPS + b * 8), :] * term[j]
            out_ref[rows, :] = value
        return carry

    lax.fori_loop(0, 8, step, 0)


def finish(base, coupling, scale, dense):
    return pl.pallas_call(
        finish_kernel,
        out_shape=f32_rows(ROWS),
        in_specs=[VMEM] * 4,
        out_specs=VMEM,
        compiler_params=params(),
        cost_estimate=cost(600000, 2000000),
        name="finish",
    )(base, coupling, scale, dense)


def local(
    psi_start, objective, jacobian, precond, volume, counts, neighbours, donor, match_block, slide
):
    by_core = [[2 * chip + core for chip in range(CHIPS)] for core in range(2)]
    swap_core = [(i, i ^ 1) for i in range(NT)]

    def across(x):
        moved = lax.all_to_all(x.reshape(CHIPS, CHUNK, 128), "tm", 0, 0, axis_index_groups=by_core)
        return moved.reshape(ROWS, 128)
    def blk_swap(x, bits):
        return lax.ppermute(x, "blk", [(i, i ^ bits) for i in range(8)])

    psi = psi_start.reshape(ROWS, 128)
    target = objective.reshape(ROWS, 128)
    faces = donor.reshape(4, 128)
    dense, stencil, live, scale, route = prepare(
        counts, match_block.reshape(4), slide.reshape(4),
        precond[0, 0], neighbours.reshape(ROWS, 128), volume.reshape(GROUPS, 128)
    )
    for sweep in range(SWEEPS):
        states = across(psi)
        sent = pack_donors(sweep == 0, psi, faces)
        near = merge(sent, *[blk_swap(sent, 2 * hop) for hop in (1, 2, 3)])
        states, near, dense = lax.optimization_barrier((states, near, dense))
        coupling = across(couple(states, lax.ppermute(states, "tm", swap_core)))
        far = blk_swap(near, 1)
        base = flux_part(psi, target, jacobian[0, 0], near, far, route, live, stencil, dense)
        psi = finish(base, coupling, scale, dense)
    return psi.reshape(1, 1, F, CELLS)


def solution(mesh):
    in_specs = (
        P("tm", "blk", None, None),
        P("tm", "blk", None, None),
        P("tm", "blk", None, None, None, None),
        P("tm", "blk", None, None, None),
        P("blk", None),
        P("blk"),
        P("blk", None, None),
        P("blk", None),
        P("tm", "blk", None),
        P("tm", "blk", None),
    )
    out_specs = P("tm", "blk", None, None)
    return jax.shard_map(local, mesh=mesh, in_specs=in_specs, out_specs=out_specs, check_vma=False)
```

time: 192 us -> 78.9 us (0.41)
  the two profiles are of different devices: /device:TPU:1 before, /device:TPU:32 now
where the time goes in v1:
time: 78.9 us; the launch traced here: 78.3 us
  starting transfers between devices  35.4 us (45%)
  waiting for transfers between devices  22.9 us (29%)
  Pallas kernels  18.3 us (23%)
  between operations  0.86 us (1%)
  local copies, waits for them, and re-layouts  0.85 us (1%)
    all_to_all x4, waiting for transfers between devices, across(): lax.all_to_all(x.reshape(CHIPS, CHUNK, 128), 'tm', 0, 0, axis_index_group...  22.8 us
    all_to_all x4, starting transfers between devices, across(): lax.all_to_all(x.reshape(CHIPS, CHUNK, 128), 'tm', 0, 0, axis_index_group...  22.2 us
    ppermute x8, starting transfers between devices, blk_swap(): return lax.ppermute(x, 'blk', [(i, i ^ bits) for i in range(8)])  13.2 us
    pallas_call x2, Pallas kernels, flux_part(): pl.pallas_call(flux_kernel, out_shape=f32_rows(ROWS), in_specs=[ANY] * 3...  7.49 us
    pallas_call x1, Pallas kernels, prepare(): pl.pallas_call(prepare_kernel, out_shape=(f32_rows(F * F * GROUPS), i32_r...  3.73 us
    pallas_call x2, Pallas kernels, pack_donors(): pl.pallas_call(fetch_donor_kernel if fetch else donor_kernel, out_shape=f...  3.02 us
    pallas_call x2, Pallas kernels, couple(): pl.pallas_call(couple_kernel, out_shape=f32_rows(ROWS), in_specs=[VMEM, V...  2.19 us
    pallas_call x2, Pallas kernels, finish(): pl.pallas_call(finish_kernel, out_shape=f32_rows(ROWS), in_specs=[VMEM] *...  1.85 us
  transfers between devices with their start and end apart: 14, of which 4 were waited for; matrix products, arithmetic and copies ran while one was open for 0% of the time, Pallas kernels for 17%

profile of v1, /device:TPU:32, one launch (start us, length us, event | category | flops | bytes accessed | tf_op | source)
XLA Modules:
  0.0 78.3 jit_solution(15507726544385660159)
XLA Ops:
  0.0 1.8 %pack_donors.2.refs_0_ = f32[32,128]{1,0:T(8,128)} custom-call(f32[384,128]{1,0:T(8,128)} %bitcast.20, s32[4,128]{1,0:T(4,128)} %bitcast.27), custom_call_target="tpu_custom_call" | custom-call | flops 400000 | bytes 220000 | tf_op jit(solution)/shard_map/pack_donors/pallas_call | solution.py:90
  1.8 2.8 %collective-permute-start.2 = (f32[32,128]{1,0:T(8,128)}, f32[32,128]{1,0:T(8,128)S(1)}, u32[]{:S(2)}, u32[]{:S(2)}) collective-permute-start(f32[32,128]{1,0:T(8,128)} %pack_donors.2.refs_0_), channel_id=1, source_target_pairs={{0,6},{1,7},{2,4},{3,5},{4,2},{5,3},{6,0},{7,1},{8,14},{9,15},{10,... | collective-permute-start | bytes 49160 | tf_op jit(solution)/shard_map/ppermute | solution.py:354
  4.7 0.8 %collective-permute-start.1 = (f32[32,128]{1,0:T(8,128)}, f32[32,128]{1,0:T(8,128)S(1)}, u32[]{:S(2)}, u32[]{:S(2)}) collective-permute-start(f32[32,128]{1,0:T(8,128)} %pack_donors.2.refs_0_), channel_id=1, source_target_pairs={{0,4},{1,5},{2,6},{3,7},{4,0},{5,1},{6,2},{7,3},{8,12},{9,13},{10,... | collective-permute-start | bytes 49160 | tf_op jit(solution)/shard_map/ppermute | solution.py:354
  5.5 0.5 collective-permute-start
  6.0 9.6 %all-to-all-start = ((f32[16,24,128]{2,1,0:T(8,128)}), f32[16,24,128]{2,1,0:T(8,128)S(1)}, u32[]{:S(2)}, u32[]{:S(2)}) async-start(f32[16,24,128]{2,1,0:T(8,128)} %bitcast.21), calls=%async_computation | async-start | bytes 393216 | tf_op jit(solution)/shard_map/all_to_all | solution.py:351
  16.3 0.0 copy-start.6
  16.3 3.7 %prepare.1 = (f32[2304,128]{1,0:T(8,128)}, s32[512,128]{1,0:T(8,128)}, f32[64,128]{1,0:T(8,128)}, f32[64,128]{1,0:T(8,128)}, s32[16,128]{1,0:T(8,128)}) custom-call(s32[1]{0:T(128)S(6)} %copy.13.counts_hbm, s32[4]{0:T(128)} %bitcast.34, s32[4]{0:T(128)} %bitcast.35, bf16[6,6,8192]{2,1,0:T(8,128)(2,1)} %bitcast.31, s32[384,128]{1,0:T(8,128)} %bitcast.32, ...), custom_call_target="tpu_custom_call" | custom-call | flops 1000000 | bytes 2500000 | tf_op jit(solution)/shard_map/prepare/pallas_call | solution.py:174
  20.0 0.0 copy-start
  20.0 0.0 copy-start.1
  20.0 0.0 collective-permute-done.2.refs_3_
  20.1 0.0 collective-permute-done.1.refs_2_
  20.1 0.0 collective-permute-done.refs_1_
  20.1 0.0 copy-start.3
  20.1 0.8 %copy-done.3 = f32[32,128]{1,0:T(8,128)S(1)} copy-done((f32[32,128]{1,0:T(8,128)S(1)}, f32[32,128]{1,0:T(8,128)}, u32[]{:S(2)}) %copy-start.3) | copy-done | bytes 16408
  20.9 0.0 copy-start.5
  20.9 0.0 copy-start.7
  20.9 0.0 copy-start.8
  20.9 3.1 %all-to-all-done = f32[16,24,128]{2,1,0:T(8,128)S(1)} async-done(((f32[16,24,128]{2,1,0:T(8,128)}), f32[16,24,128]{2,1,0:T(8,128)S(1)}, u32[]{:S(2)}, u32[]{:S(2)}) %all-to-all-start) | async-done | bytes 196640 | tf_op jit(solution)/shard_map/all_to_all | solution.py:351
  24.1 0.0 collective-permute-start.4
  24.1 2.9 %collective-permute-start.3 = (f32[128,128]{1,0:T(8,128)S(1)}, f32[128,128]{1,0:T(8,128)S(1)}, u32[]{:S(2)}, u32[]{:S(2)}) collective-permute-start(f32[128,128]{1,0:T(8,128)S(1)} %merge.2.near_ref), channel_id=1, source_target_pairs={{0,1},{1,0},{2,3},{3,2},{4,5},{5,4},{6,7},{7,6},{8,9},{9,8},{10,11... | collective-permute-start | bytes 196616 | tf_op jit(solution)/shard_map/ppermute | solution.py:354
  27.0 0.0 collective-permute-done.4.other_ref
  27.0 1.1 %couple.2 = f32[384,128]{1,0:T(8,128)} custom-call(f32[384,128]{1,0:T(8,128)S(1)} %bitcast.24, f32[384,128]{1,0:T(8,128)S(1)} %collective-permute-done.4.other_ref), custom_call_target="tpu_custom_call" | custom-call | flops 3200000 | bytes 600000 | tf_op jit(solution)/shard_map/couple/pallas_call | solution.py:306
  28.1 4.6 %all-to-all-start.1 = ((f32[16,24,128]{2,1,0:T(8,128)}), f32[16,24,128]{2,1,0:T(8,128)S(1)}, u32[]{:S(2)}, u32[]{:S(2)}) async-start(f32[16,24,128]{2,1,0:T(8,128)} %bitcast.11), calls=%async_computation.1 | async-start | bytes 393216 | tf_op jit(solution)/shard_map/all_to_all | solution.py:351
  32.6 0.0 collective-permute-done.3.far_ref
  32.6 0.0 copy-done.6
  32.6 0.0 copy-done
  32.7 0.0 copy-done.1
  32.7 0.0 copy-done.5
  32.7 0.0 copy-done.7
  32.7 0.0 copy-done.8
  32.7 0.0 copy-start.2
  32.7 0.0 copy-start.4
  32.7 3.8 %flux_part.2.base_ref = f32[384,128]{1,0:T(8,128)S(1)} custom-call(f32[384,128]{1,0:T(8,128)S(1)} %bitcast.22, f32[384,128]{1,0:T(8,128)S(1)} %bitcast.29, bf16[6,6,6,8192]{3,2,1,0:T(8,128)(2,1)} %bitcast.36, f32[128,128]{1,0:T(8,128)S(1)} %merge.2.near_ref, f32[128,128]{1,0:T(8,128)S(1)} %collective-permute-done.3.far_ref, s32[16,128]{1,0:T(8,128)S(1)} %copy-done.8, ...), custom_call_target="tpu_custom_call" | custom-call | flops 30000001024 | bytes 7000000 | tf_op jit(solution)/shard_map/flux_part/pallas_call | solution.py:267
  36.5 5.3 %all-to-all-done.1 = f32[16,24,128]{2,1,0:T(8,128)S(1)} async-done(((f32[16,24,128]{2,1,0:T(8,128)}), f32[16,24,128]{2,1,0:T(8,128)S(1)}, u32[]{:S(2)}, u32[]{:S(2)}) %all-to-all-start.1) | async-done | bytes 196640 | tf_op jit(solution)/shard_map/all_to_all | solution.py:351
  41.8 0.0 copy-done.2
  41.8 0.9 %finish.2.psi_ref.psi_hbm = f32[384,128]{1,0:T(8,128)} custom-call(f32[384,128]{1,0:T(8,128)S(1)} %flux_part.2.base_ref, f32[384,128]{1,0:T(8,128)S(1)} %bitcast.19, f32[64,128]{1,0:T(8,128)S(1)} %copy-done.2, f32[2304,128]{1,0:T(8,128)S(1)} %copy-done), custom_call_target="tpu_custom_call" | custom-call | flops 600000 | bytes 2000000 | tf_op jit(solution)/shard_map/finish/pallas_call | solution.py:333
  42.8 0.0 copy-done.4
  42.8 1.2 %pack_donors.3.refs_0_ = f32[32,128]{1,0:T(8,128)S(1)} custom-call(f32[384,128]{1,0:T(8,128)} %finish.2.psi_ref.psi_hbm, s32[4,128]{1,0:T(4,128)S(1)} %bitcast.28), custom_call_target="tpu_custom_call" | custom-call | flops 400000 | bytes 220000 | tf_op jit(solution)/shard_map/pack_donors/pallas_call | solution.py:90
  44.0 2.8 %collective-permute-start.7 = (f32[32,128]{1,0:T(8,128)S(1)}, f32[32,128]{1,0:T(8,128)S(1)}, u32[]{:S(2)}, u32[]{:S(2)}) collective-permute-start(f32[32,128]{1,0:T(8,128)S(1)} %pack_donors.3.refs_0_), channel_id=1, source_target_pairs={{0,6},{1,7},{2,4},{3,5},{4,2},{5,3},{6,0},{7,1},{8,14},{9,15},{10,... | collective-permute-start | bytes 49160 | tf_op jit(solution)/shard_map/ppermute | solution.py:354
  46.8 0.8 %collective-permute-start.6 = (f32[32,128]{1,0:T(8,128)S(1)}, f32[32,128]{1,0:T(8,128)S(1)}, u32[]{:S(2)}, u32[]{:S(2)}) collective-permute-start(f32[32,128]{1,0:T(8,128)S(1)} %pack_donors.3.refs_0_), channel_id=1, source_target_pairs={{0,4},{1,5},{2,6},{3,7},{4,0},{5,1},{6,2},{7,3},{8,12},{9,13},{10,... | collective-permute-start | bytes 49160 | tf_op jit(solution)/shard_map/ppermute | solution.py:354
  47.6 0.5 collective-permute-start.5
  48.2 4.3 %all-to-all-start.2 = ((f32[16,24,128]{2,1,0:T(8,128)}), f32[16,24,128]{2,1,0:T(8,128)S(1)}, u32[]{:S(2)}, u32[]{:S(2)}) async-start(f32[16,24,128]{2,1,0:T(8,128)} %bitcast.13), calls=%async_computation.2 | async-start | bytes 393216 | tf_op jit(solution)/shard_map/all_to_all | solution.py:351
  52.5 0.0 collective-permute-done.7.refs_3_
  52.5 0.0 collective-permute-done.6.refs_2_
  52.5 0.0 collective-permute-done.5.refs_1_
  52.5 8.5 %all-to-all-done.2 = f32[16,24,128]{2,1,0:T(8,128)S(1)} async-done(((f32[16,24,128]{2,1,0:T(8,128)}), f32[16,24,128]{2,1,0:T(8,128)S(1)}, u32[]{:S(2)}, u32[]{:S(2)}) %all-to-all-start.2) | async-done | bytes 196640 | tf_op jit(solution)/shard_map/all_to_all | solution.py:351
  61.0 0.0 collective-permute-start.9
  61.0 1.9 %collective-permute-start.8 = (f32[128,128]{1,0:T(8,128)S(1)}, f32[128,128]{1,0:T(8,128)S(1)}, u32[]{:S(2)}, u32[]{:S(2)}) collective-permute-start(f32[128,128]{1,0:T(8,128)S(1)} %merge.3.near_ref), channel_id=1, source_target_pairs={{0,1},{1,0},{2,3},{3,2},{4,5},{5,4},{6,7},{7,6},{8,9},{9,8},{10,11... | collective-permute-start | bytes 196616 | tf_op jit(solution)/shard_map/ppermute | solution.py:354
  62.9 0.0 collective-permute-done.9.other_ref
  62.9 1.1 %couple.3 = f32[384,128]{1,0:T(8,128)} custom-call(f32[384,128]{1,0:T(8,128)S(1)} %bitcast.26, f32[384,128]{1,0:T(8,128)S(1)} %collective-permute-done.9.other_ref), custom_call_target="tpu_custom_call" | custom-call | flops 3200000 | bytes 600000 | tf_op jit(solution)/shard_map/couple/pallas_call | solution.py:306
  64.0 3.7 %all-to-all-start.3 = ((f32[16,24,128]{2,1,0:T(8,128)}), f32[16,24,128]{2,1,0:T(8,128)S(1)}, u32[]{:S(2)}, u32[]{:S(2)}) async-start(f32[16,24,128]{2,1,0:T(8,128)} %bitcast.15), calls=%async_computation.3 | async-start | bytes 393216 | tf_op jit(solution)/shard_map/all_to_all | solution.py:351
  67.8 0.0 collective-permute-done.8.far_ref
  67.8 3.7 %flux_part.3.base_ref = f32[384,128]{1,0:T(8,128)S(1)} custom-call(f32[384,128]{1,0:T(8,128)} %finish.2.psi_ref.psi_hbm, f32[384,128]{1,0:T(8,128)S(1)} %bitcast.30, bf16[6,6,6,8192]{3,2,1,0:T(8,128)(2,1)} %bitcast.37, f32[128,128]{1,0:T(8,128)S(1)} %merge.3.near_ref, f32[128,128]{1,0:T(8,128)S(1)} %collective-permute-done.8.far_ref, ...), custom_call_target="tpu_custom_call" | custom-call | flops 30000001024 | bytes 7000000 | tf_op jit(solution)/shard_map/flux_part/pallas_call | solution.py:267
  71.5 5.9 %all-to-all-done.3 = f32[16,24,128]{2,1,0:T(8,128)S(1)} async-done(((f32[16,24,128]{2,1,0:T(8,128)}), f32[16,24,128]{2,1,0:T(8,128)S(1)}, u32[]{:S(2)}, u32[]{:S(2)}) %all-to-all-start.3) | async-done | bytes 196640 | tf_op jit(solution)/shard_map/all_to_all | solution.py:351
  77.3 0.9 %finish.3 = f32[384,128]{1,0:T(8,128)} custom-call(f32[384,128]{1,0:T(8,128)S(1)} %flux_part.3.base_ref, f32[384,128]{1,0:T(8,128)S(1)} %bitcast.18, f32[64,128]{1,0:T(8,128)S(1)} %copy-done.2, f32[2304,128]{1,0:T(8,128)S(1)} %copy-done), custom_call_target="tpu_custom_call" | custom-call | flops 600000 | bytes 2000000 | tf_op jit(solution)/shard_map/finish/pallas_call | solution.py:333
  (2 shorter events, 0.0 us)
Async XLA Ops:
  1.8 18.2 %collective-permute-start.2 = (f32[32,128]{1,0:T(8,128)}, f32[32,128]{1,0:T(8,128)S(1)}, u32[]{:S(2)}, u32[]{:S(2)}) collective-permute-start(f32[32,128]{1,0:T(8,128)} %pack_donors.2.refs_0_), channel_id=1, source_target_pairs={{0,6},{1,7},{2,4},{3,5},{4,2},{5,3},{6,0},{7,1},{8,14},{9,15},{10,... | collective-permute-start | bytes 49160 | tf_op jit(solution)/shard_map/ppermute | solution.py:354
  4.7 15.4 %collective-permute-start.1 = (f32[32,128]{1,0:T(8,128)}, f32[32,128]{1,0:T(8,128)S(1)}, u32[]{:S(2)}, u32[]{:S(2)}) collective-permute-start(f32[32,128]{1,0:T(8,128)} %pack_donors.2.refs_0_), channel_id=1, source_target_pairs={{0,4},{1,5},{2,6},{3,7},{4,0},{5,1},{6,2},{7,3},{8,12},{9,13},{10,... | collective-permute-start | bytes 49160 | tf_op jit(solution)/shard_map/ppermute | solution.py:354
  5.5 14.6 %collective-permute-start = (f32[32,128]{1,0:T(8,128)}, f32[32,128]{1,0:T(8,128)S(1)}, u32[]{:S(2)}, u32[]{:S(2)}) collective-permute-start(f32[32,128]{1,0:T(8,128)} %pack_donors.2.refs_0_), channel_id=1, source_target_pairs={{0,2},{1,3},{2,0},{3,1},{4,6},{5,7},{6,4},{7,5},{8,10},{9,11},{10,... | collective-permute-start | bytes 49160 | tf_op jit(solution)/shard_map/ppermute | solution.py:354
  6.0 18.0 %all-to-all-start = ((f32[16,24,128]{2,1,0:T(8,128)}), f32[16,24,128]{2,1,0:T(8,128)S(1)}, u32[]{:S(2)}, u32[]{:S(2)}) async-start(f32[16,24,128]{2,1,0:T(8,128)} %bitcast.21), calls=%async_computation | async-start | bytes 393216 | tf_op jit(solution)/shard_map/all_to_all | solution.py:351
  16.3 16.4 %copy-start.6 = (f32[1,1,6,8192]{3,1,2,0:T(1,128)S(1)}, f32[1,1,6,8192]{3,1,2,0:T(1,128)}, u32[]{:S(2)}) copy-start(f32[1,1,6,8192]{3,1,2,0:T(1,128)} %param.11) | copy-start | bytes 589828
  20.0 12.6 %copy-start = (f32[2304,128]{1,0:T(8,128)S(1)}, f32[2304,128]{1,0:T(8,128)}, u32[]{:S(2)}) copy-start(f32[2304,128]{1,0:T(8,128)} %get-tuple-element.25.dense_ref) | copy-start | bytes 3538948
  20.0 12.6 %copy-start.1 = (f32[1,1,6,8192]{3,1,2,0:T(1,128)S(1)}, f32[1,1,6,8192]{3,1,2,0:T(1,128)}, u32[]{:S(2)}) copy-start(f32[1,1,6,8192]{3,1,2,0:T(1,128)} %param.10) | copy-start | bytes 589828
  20.1 0.8 %copy-start.3 = (f32[32,128]{1,0:T(8,128)S(1)}, f32[32,128]{1,0:T(8,128)}, u32[]{:S(2)}) copy-start(f32[32,128]{1,0:T(8,128)} %pack_donors.2.refs_0_) | copy-start | bytes 49156
  20.9 11.8 %copy-start.5 = (s32[512,128]{1,0:T(8,128)S(1)}, s32[512,128]{1,0:T(8,128)}, u32[]{:S(2)}) copy-start(s32[512,128]{1,0:T(8,128)} %get-tuple-element.20.stencil_ref) | copy-start | bytes 786436
  20.9 11.8 %copy-start.7 = (f32[64,128]{1,0:T(8,128)S(1)}, f32[64,128]{1,0:T(8,128)}, u32[]{:S(2)}) copy-start(f32[64,128]{1,0:T(8,128)} %get-tuple-element.19.live_ref) | copy-start | bytes 98308
  20.9 11.8 %copy-start.8 = (s32[16,128]{1,0:T(8,128)S(1)}, s32[16,128]{1,0:T(8,128)}, u32[]{:S(2)}) copy-start(s32[16,128]{1,0:T(8,128)} %get-tuple-element.18.route_ref) | copy-start | bytes 24580
  24.1 2.9 %collective-permute-start.4 = (f32[384,128]{1,0:T(8,128)S(1)}, f32[384,128]{1,0:T(8,128)S(1)}, u32[]{:S(2)}, u32[]{:S(2)}) collective-permute-start(f32[384,128]{1,0:T(8,128)S(1)} %bitcast.23), channel_id=1, source_target_pairs={{0,8},{8,0},{16,24},{24,16},{32,40},{40,32},{48,56},{56,48},{64,72... | collective-permute-start | bytes 589832 | tf_op jit(solution)/shard_map/ppermute | solution.py:368
  24.1 8.6 %collective-permute-start.3 = (f32[128,128]{1,0:T(8,128)S(1)}, f32[128,128]{1,0:T(8,128)S(1)}, u32[]{:S(2)}, u32[]{:S(2)}) collective-permute-start(f32[128,128]{1,0:T(8,128)S(1)} %merge.2.near_ref), channel_id=1, source_target_pairs={{0,1},{1,0},{2,3},{3,2},{4,5},{5,4},{6,7},{7,6},{8,9},{9,8},{10,11... | collective-permute-start | bytes 196616 | tf_op jit(solution)/shard_map/ppermute | solution.py:354
  28.1 13.8 %all-to-all-start.1 = ((f32[16,24,128]{2,1,0:T(8,128)}), f32[16,24,128]{2,1,0:T(8,128)S(1)}, u32[]{:S(2)}, u32[]{:S(2)}) async-start(f32[16,24,128]{2,1,0:T(8,128)} %bitcast.11), calls=%async_computation.1 | async-start | bytes 393216 | tf_op jit(solution)/shard_map/all_to_all | solution.py:351
  32.7 9.2 %copy-start.2 = (f32[64,128]{1,0:T(8,128)S(1)}, f32[64,128]{1,0:T(8,128)}, u32[]{:S(2)}) copy-start(f32[64,128]{1,0:T(8,128)} %get-tuple-element.23.scale_ref) | copy-start | bytes 98308
  32.7 10.1 %copy-start.4 = (s32[1,512]{1,0:T(1,128)S(1)}, s32[1,512]{1,0:T(1,128)}, u32[]{:S(2)}) copy-start(s32[1,512]{1,0:T(1,128)} %param.17) | copy-start | bytes 6148
  44.0 8.5 %collective-permute-start.7 = (f32[32,128]{1,0:T(8,128)S(1)}, f32[32,128]{1,0:T(8,128)S(1)}, u32[]{:S(2)}, u32[]{:S(2)}) collective-permute-start(f32[32,128]{1,0:T(8,128)S(1)} %pack_donors.3.refs_0_), channel_id=1, source_target_pairs={{0,6},{1,7},{2,4},{3,5},{4,2},{5,3},{6,0},{7,1},{8,14},{9,15},{10,... | collective-permute-start | bytes 49160 | tf_op jit(solution)/shard_map/ppermute | solution.py:354
  46.8 5.7 %collective-permute-start.6 = (f32[32,128]{1,0:T(8,128)S(1)}, f32[32,128]{1,0:T(8,128)S(1)}, u32[]{:S(2)}, u32[]{:S(2)}) collective-permute-start(f32[32,128]{1,0:T(8,128)S(1)} %pack_donors.3.refs_0_), channel_id=1, source_target_pairs={{0,4},{1,5},{2,6},{3,7},{4,0},{5,1},{6,2},{7,3},{8,12},{9,13},{10,... | collective-permute-start | bytes 49160 | tf_op jit(solution)/shard_map/ppermute | solution.py:354
  47.6 4.9 %collective-permute-start.5 = (f32[32,128]{1,0:T(8,128)S(1)}, f32[32,128]{1,0:T(8,128)S(1)}, u32[]{:S(2)}, u32[]{:S(2)}) collective-permute-start(f32[32,128]{1,0:T(8,128)S(1)} %pack_donors.3.refs_0_), channel_id=1, source_target_pairs={{0,2},{1,3},{2,0},{3,1},{4,6},{5,7},{6,4},{7,5},{8,10},{9,11},{10,... | collective-permute-start | bytes 49160 | tf_op jit(solution)/shard_map/ppermute | solution.py:354
  48.2 12.9 %all-to-all-start.2 = ((f32[16,24,128]{2,1,0:T(8,128)}), f32[16,24,128]{2,1,0:T(8,128)S(1)}, u32[]{:S(2)}, u32[]{:S(2)}) async-start(f32[16,24,128]{2,1,0:T(8,128)} %bitcast.13), calls=%async_computation.2 | async-start | bytes 393216 | tf_op jit(solution)/shard_map/all_to_all | solution.py:351
  61.0 1.9 %collective-permute-start.9 = (f32[384,128]{1,0:T(8,128)S(1)}, f32[384,128]{1,0:T(8,128)S(1)}, u32[]{:S(2)}, u32[]{:S(2)}) collective-permute-start(f32[384,128]{1,0:T(8,128)S(1)} %bitcast.25), channel_id=1, source_target_pairs={{0,8},{8,0},{16,24},{24,16},{32,40},{40,32},{48,56},{56,48},{64,72... | collective-permute-start | bytes 589832 | tf_op jit(solution)/shard_map/ppermute | solution.py:368
  61.0 6.8 %collective-permute-start.8 = (f32[128,128]{1,0:T(8,128)S(1)}, f32[128,128]{1,0:T(8,128)S(1)}, u32[]{:S(2)}, u32[]{:S(2)}) collective-permute-start(f32[128,128]{1,0:T(8,128)S(1)} %merge.3.near_ref), channel_id=1, source_target_pairs={{0,1},{1,0},{2,3},{3,2},{4,5},{5,4},{6,7},{7,6},{8,9},{9,8},{10,11... | collective-permute-start | bytes 196616 | tf_op jit(solution)/shard_map/ppermute | solution.py:354
  64.0 13.3 %all-to-all-start.3 = ((f32[16,24,128]{2,1,0:T(8,128)}), f32[16,24,128]{2,1,0:T(8,128)S(1)}, u32[]{:S(2)}, u32[]{:S(2)}) async-start(f32[16,24,128]{2,1,0:T(8,128)} %bitcast.15), calls=%async_computation.3 | async-start | bytes 393216 | tf_op jit(solution)/shard_map/all_to_all | solution.py:351
